TPU v7x, 32 devices: a whole 2x2x4 slice. The times are simulated.
32 devices in a mesh: parts: 2 (over y), replica: 4 (over x, core), tensor: 4 (over z).
Axes of the slice: x: 2, y: 2, z: 4, core: 2. Of those that a mesh axis runs over, the one named last changes fastest.
Arguments:
- embedded: bfloat16 [8, 128, 5120], P(None, ('parts', 'replica'), 'tensor'), parts along dimension 1, may hold values from -500 to 500
- w_query: bfloat16 [5120, 4096], P(None, 'tensor'), may hold values from -0.078125 to 0.078125
- w_key: bfloat16 [5120, 512], P(None, 'tensor'), may hold values from -0.078125 to 0.078125
- w_value: bfloat16 [5120, 512], P(None, 'tensor'), may hold values from -0.078125 to 0.078125
- w_out: bfloat16 [4096, 5120], P(None, 'tensor'), may hold values from -0.09375 to 0.09375
- prefix_cache: bfloat16 [32, 2048, 1024], P(('parts', 'replica'), 'tensor'), parts along dimension 0, may hold values from -70 to 70
- prefix_len: int32 [32], P(('parts', 'replica')), parts along dimension 0, may hold values from 1 to 2048, as said below
- child_parent: int32 [128], P(('parts', 'replica')), parts along dimension 0, may hold values from 0 to 15, as said below
Outputs:
- attn_out: bfloat16 [8, 128, 5120], P(None, ('parts', 'replica'), 'tensor'), parts along dimension 1
There are 2 independent parts, one for each index of `parts`. A program takes and returns all parts, laid end to end along the dimension named above; an argument that names none is the same for every part. Nothing has to cross between parts.
Inputs may be any that keep to these rules, and one draw needn't show every extreme that they name: `child_parent`: parent p lives on replica p // 4; every child slot names a parent on another replica; the child slots of one replica name exactly 2 distinct parents of each other replica. `prefix_len`: one parent in every part has the full 2048.
All inputs are finite; a program needn't handle non-finite values.
Results may differ from a plain program's by a relative error of at most 0.025.
Values may be sent and summed in bfloat16 or wider, within the bound.
A program may use at most 320 MiB of HBM per device.

v0:
```python
import jax
import jax.numpy as jnp
from jax import lax
from jax.sharding import PartitionSpec as P

HEADS = 32
KV_HEADS = 4
HEAD = 128


EPS = 1e-06
NEG = -1e30
ROPE_BASE = 1000000.0


def combined_all(x, axis, combine):
    everything = jax.tree.map(
        lambda part, kind: lax.all_gather(part.astype(kind), axis),
        x,
        (jnp.bfloat16, jnp.bfloat16, jnp.bfloat16),
    )

    def take(k):
        return jax.tree.map(lambda part, own: part[k].astype(own.dtype), everything, x)

    return lax.fori_loop(
        1, lax.axis_size(axis), lambda k, so_far: combine(so_far, take(k)), take(0)
    )


def rotate(values, positions):
    half = values.shape[-1] // 2
    freq = ROPE_BASE ** (-jnp.arange(half, dtype=jnp.float32) / half)
    angle = positions.astype(jnp.float32)[..., None] * freq
    cosine = jnp.cos(angle)
    sine = jnp.sin(angle)
    first = values[..., :half]
    second = values[..., half:]
    return jnp.concatenate(
        [first * cosine - second * sine, first * sine + second * cosine], axis=-1
    )


def combine(first, second):
    upper = jnp.maximum(first[0], second[0])
    left = jnp.exp(first[0] - upper)
    right = jnp.exp(second[0] - upper)
    return (
        upper,
        first[1] * left + second[1] * right,
        first[2] * left[..., None] + second[2] * right[..., None],
    )


def rms_normed(current):
    whole = current.astype(jnp.float32)
    return (whole * lax.rsqrt(jnp.mean(whole * whole, axis=-1, keepdims=True) + EPS)).astype(
        jnp.bfloat16
    )


def per_device(embedded, w_query, w_key, w_value, w_out, prefix_cache, prefix_len, child_parent):
    steps = embedded.shape[0]
    rows = embedded.shape[1]
    par_dev, pos_dev, width = prefix_cache.shape
    kv_width = width // 2
    group = HEADS // KV_HEADS
    scale = HEAD ** (-0.5)
    table = lax.all_gather(prefix_cache, "replica", axis=0, tiled=True)
    lengths_all = lax.all_gather(prefix_len, "replica", axis=0, tiled=True)
    lengths = lengths_all[child_parent]
    chosen = jnp.take(table, child_parent, axis=0)
    keys = jnp.transpose(
        chosen[:, :, :kv_width].reshape(rows, pos_dev, KV_HEADS, HEAD), (0, 2, 1, 3)
    )
    values = jnp.transpose(
        chosen[:, :, kv_width:].reshape(rows, pos_dev, KV_HEADS, HEAD), (0, 2, 1, 3)
    )
    positions = lax.axis_index("tensor") * pos_dev + jnp.arange(pos_dev, dtype=jnp.int32)
    valid = positions[None, :] < lengths[:, None]
    block_mask = valid[:, None, None, :]
    features = jnp.stack(
        [lax.all_gather(embedded[step], "tensor", axis=1, tiled=True) for step in range(steps)],
        axis=0,
    )
    normed = rms_normed(features).reshape(steps * rows, -1)
    position = lengths[None, :] + jnp.arange(steps, dtype=jnp.int32)[:, None]
    query_part = jnp.dot(normed, w_query, preferred_element_type=jnp.float32)
    local_heads = query_part.shape[1] // HEAD
    query_part = (
        rotate(query_part.reshape(steps, rows, local_heads, HEAD), position[:, :, None])
        .reshape(steps, rows, local_heads * HEAD)
        .astype(jnp.bfloat16)
    )
    key_part = (
        jnp.dot(normed, w_key, preferred_element_type=jnp.float32)
        .astype(jnp.bfloat16)
        .reshape(steps, rows, -1)
    )
    value_part = (
        jnp.dot(normed, w_value, preferred_element_type=jnp.float32)
        .astype(jnp.bfloat16)
        .reshape(steps, rows, -1)
    )
    query_all, key_all, value_all = (
        lax.all_gather(query_part, "tensor", axis=2, tiled=True),
        lax.all_gather(key_part, "tensor", axis=2, tiled=True),
        lax.all_gather(value_part, "tensor", axis=2, tiled=True),
    )
    own_keys = rotate(
        key_all.astype(jnp.float32).reshape(steps, rows, KV_HEADS, HEAD), position[:, :, None]
    ).astype(jnp.bfloat16)
    own_values = value_all.reshape(steps, rows, KV_HEADS, HEAD)
    queries = query_all.reshape(steps, rows, KV_HEADS, group, HEAD)
    scores = (
        jnp.einsum("sckgd,ckpd->sckgp", queries, keys, preferred_element_type=jnp.float32) * scale
    )
    full_mask = block_mask[None]
    scores = jnp.where(full_mask, scores, NEG)
    upper = jnp.max(scores, axis=-1)
    weights = jnp.where(full_mask, jnp.exp(scores - upper[..., None]), 0.0)
    total = jnp.sum(weights, axis=-1)
    partial_value = jnp.einsum(
        "sckgp,ckpd->sckgd",
        weights.astype(jnp.bfloat16),
        values,
        preferred_element_type=jnp.float32,
    )
    merged = combined_all((upper, total, partial_value), "tensor", combine)
    causal = (jnp.arange(steps)[None, :] <= jnp.arange(steps)[:, None])[:, None, None, None, :]
    own_scores = (
        jnp.einsum("sckgd,tckd->sckgt", queries, own_keys, preferred_element_type=jnp.float32)
        * scale
    )
    own_scores = jnp.where(causal, own_scores, NEG)
    own_upper = jnp.max(own_scores, axis=-1)
    own_weights = jnp.where(causal, jnp.exp(own_scores - own_upper[..., None]), 0.0)
    own_total = jnp.sum(own_weights, axis=-1)
    own_partial = jnp.einsum(
        "sckgt,tckd->sckgd",
        own_weights.astype(jnp.bfloat16),
        own_values,
        preferred_element_type=jnp.float32,
    )
    final = combine(merged, (own_upper, own_total, own_partial))
    attended = (
        (final[2] / final[1][..., None]).reshape(steps * rows, HEADS * HEAD).astype(jnp.bfloat16)
    )
    result = jnp.dot(attended, w_out, preferred_element_type=jnp.float32).astype(jnp.bfloat16)
    return result.reshape(steps, rows, -1)


def solution(mesh):
    in_specs = (
        P(None, ("parts", "replica"), "tensor"),
        P(None, "tensor"),
        P(None, "tensor"),
        P(None, "tensor"),
        P(None, "tensor"),
        P(("parts", "replica"), "tensor", None),
        P(("parts", "replica")),
        P(("parts", "replica")),
    )
    out_specs = P(None, ("parts", "replica"), "tensor")
    return jax.shard_map(
        per_device, mesh=mesh, in_specs=in_specs, out_specs=out_specs, check_vma=False
    )
```

profile of v0, /device:TPU:0, one launch (start us, length us, event | category | flops | bytes accessed | tf_op | source)
XLA Modules:
  0.0 517.8 jit_solution(4903594320144872305)
XLA Ops:
  6.6 0.8 compare_select_fusion
  7.3 1.2 dynamic-slice
  9.2 0.9 dynamic-update-slice
  10.1 6.3 %all-reduce = s32[16]{0:T(128)S(1)} all-reduce(s32[16]{0:T(128)S(1)} %dynamic-update-slice), channel_id=1, replica_groups=mesh['parts'=2,'replica'=4,'tensor'=4] {'replica'}, use_global_device_ids=true, to_apply=%add | all-reduce | flops 16 | bytes 128
  16.4 0.7 gather_fusion
  17.1 1.0 fusion.56
  18.0 13.7 %all-gather.7 = bf16[1,16,5120]{2,1,0:T(8,128)(2,1)S(1)} all-gather(bf16[1,16,1280]{2,1,0:T(8,128)(2,1)S(1)} %get-tuple-element.250), channel_id=9, replica_groups=mesh['parts'=2,'replica'=4,'tensor'=4] {'tensor'}, dimensions={2}, use_global_device_ids=true | all-gather | bytes 204800 | tf_op jit(solution)/shard_map/all_gather | solution.py:83
  31.8 13.5 %all-gather.5 = bf16[1,16,5120]{2,1,0:T(8,128)(2,1)S(1)} all-gather(bf16[1,16,1280]{2,1,0:T(8,128)(2,1)S(1)} %get-tuple-element.251), channel_id=7, replica_groups=mesh['parts'=2,'replica'=4,'tensor'=4] {'tensor'}, dimensions={2}, use_global_device_ids=true | all-gather | bytes 204800 | tf_op jit(solution)/shard_map/all_gather | solution.py:83
  45.3 13.6 %all-gather.4 = bf16[1,16,5120]{2,1,0:T(8,128)(2,1)S(1)} all-gather(bf16[1,16,1280]{2,1,0:T(8,128)(2,1)S(1)} %get-tuple-element.252), channel_id=6, replica_groups=mesh['parts'=2,'replica'=4,'tensor'=4] {'tensor'}, dimensions={2}, use_global_device_ids=true | all-gather | bytes 204800 | tf_op jit(solution)/shard_map/all_gather | solution.py:83
  58.9 13.8 %all-gather.3 = bf16[1,16,5120]{2,1,0:T(8,128)(2,1)S(1)} all-gather(bf16[1,16,1280]{2,1,0:T(8,128)(2,1)S(1)} %get-tuple-element.253), channel_id=5, replica_groups=mesh['parts'=2,'replica'=4,'tensor'=4] {'tensor'}, dimensions={2}, use_global_device_ids=true | all-gather | bytes 204800 | tf_op jit(solution)/shard_map/all_gather | solution.py:83
  72.7 13.5 %all-gather.2 = bf16[1,16,5120]{2,1,0:T(8,128)(2,1)S(1)} all-gather(bf16[1,16,1280]{2,1,0:T(8,128)(2,1)S(1)} %get-tuple-element.254), channel_id=4, replica_groups=mesh['parts'=2,'replica'=4,'tensor'=4] {'tensor'}, dimensions={2}, use_global_device_ids=true | all-gather | bytes 204800 | tf_op jit(solution)/shard_map/all_gather | solution.py:83
  86.2 13.4 %all-gather.1 = bf16[1,16,5120]{2,1,0:T(8,128)(2,1)S(1)} all-gather(bf16[1,16,1280]{2,1,0:T(8,128)(2,1)S(1)} %get-tuple-element.255), channel_id=3, replica_groups=mesh['parts'=2,'replica'=4,'tensor'=4] {'tensor'}, dimensions={2}, use_global_device_ids=true | all-gather | bytes 204800 | tf_op jit(solution)/shard_map/all_gather | solution.py:83
  99.7 13.7 %all-gather = bf16[1,16,5120]{2,1,0:T(8,128)(2,1)S(1)} all-gather(bf16[1,16,1280]{2,1,0:T(8,128)(2,1)S(1)} %get-tuple-element.256), channel_id=2, replica_groups=mesh['parts'=2,'replica'=4,'tensor'=4] {'tensor'}, dimensions={2}, use_global_device_ids=true | all-gather | bytes 204800 | tf_op jit(solution)/shard_map/all_gather | solution.py:83
  113.4 13.5 %all-gather.6 = bf16[1,16,5120]{2,1,0:T(8,128)(2,1)S(1)} all-gather(bf16[1,16,1280]{2,1,0:T(8,128)(2,1)S(1)} %get-tuple-element.257), channel_id=8, replica_groups=mesh['parts'=2,'replica'=4,'tensor'=4] {'tensor'}, dimensions={2}, use_global_device_ids=true | all-gather | bytes 204800 | tf_op jit(solution)/shard_map/all_gather | solution.py:83
  127.4 13.9 %copy.133 = bf16[1024,5120]{1,0:T(8,128)(2,1)} copy(bf16[1024,5120]{0,1:T(8,128)(2,1)} %bitcast.123) | data formatting | bytes 20971520 | tf_op jit(solution)/shard_map/dot_general | solution.py:88
  141.6 6.3 %fusion.33 = f32[8,16,8,128]{3,1,2,0:T(8,128)S(1)} fusion(bf16[8,128,5120,1]{2,1,0,3:T(8,128)(2,1)} %bitcast.124, f32[8,16]{1,0:T(8,128)S(1)} %add_rsqrt_fusion, bf16[8,16,5120]{2,1,0:T(8,128)(2,1)S(1)} %constant_dynamic-update-slice_fusion), kind=kOutput, calls=%fused_computation.43 | convolution fusion | flops 1344143360 | bytes 12321280 | tf_op jit(solution)/shard_map/dot_general | solution.py:88
  148.2 0.9 copy_bitcast_fusion.1
  149.1 0.7 all-gather.15.cloned.1.call-update
  150.1 27.8 %all-gather.17.cloned.1.call-done = bf16[8,16,4096]{2,1,0:T(8,128)(2,1)} async-done(((bf16[8,16,1024]{2,1,0:T(8,128)(2,1)}), bf16[8,16,4096]{2,1,0:T(8,128)(2,1)}) %all-gather.17.cloned.1.call-update) | async-done | bytes 1048592 | tf_op jit(solution)/shard_map/all_gather | solution.py:106
  177.9 1.4 copy.142
  179.3 105.5 %all-gather.15.cloned.1.call-done = bf16[16,512,1024]{2,1,0:T(8,128)(2,1)} async-done(((bf16[4,512,1024]{2,1,0:T(8,128)(2,1)}), bf16[16,512,1024]{2,1,0:T(8,128)(2,1)}) %all-gather.15.cloned.1.call-update) | async-done | bytes 16777232 | tf_op jit(solution)/shard_map/all_gather | solution.py:69
  284.9 13.0 %gather_fusion.1 = bf16[16,512,1024]{2,1,0:T(8,128)(2,1)} fusion(bf16[16,512,1024]{2,1,0:T(8,128)(2,1)} %all-gather.15.cloned.1.call-done, s32[1024]{0:T(1024)S(1)} %pad_clamp_fusion), kind=kCustom, calls=%fused_computation.1 | custom fusion | bytes 33554496 | tf_op jit(solution)/shard_map/jit(_take)/gather | solution.py:72
  297.9 8.5 %broadcast_select_fusion = bf16[16,512,1024]{2,1,0:T(8,128)(2,1)S(1)} fusion(bf16[16,512,1024]{2,1,0:T(8,128)(2,1)} %gather_fusion.1, pred[16]{0:T(512)(128)(4,1)S(1)} %compare_and_fusion), kind=kLoop, calls=%fused_computation.12 | loop fusion | flops 8388608 | bytes 33554448 | tf_op jit(solution)/shard_map/jit(_take)/select_n | solution.py:72
  306.4 6.3 %fusion.55 = (bf16[16,512,512]{2,1,0:T(8,128)(2,1)}, bf16[16,512,512]{2,1,0:T(8,128)(2,1)}) fusion(bf16[16,512,1024]{2,1,0:T(8,128)(2,1)S(1)} %broadcast_select_fusion), kind=kLoop, calls=%fused_computation.97 | loop fusion | bytes 33554432 | tf_op jit(solution)/shard_map/slice | solution.py:77
  312.8 12.3 %copy.105 = bf16[16,512,512]{1,2,0:T(8,128)(2,1)} copy(bf16[16,512,512]{2,1,0:T(8,128)(2,1)} %get-tuple-element.242) | data formatting | bytes 16777216 | tf_op jit(solution)/shard_map/slice | solution.py:77
  325.1 12.3 %copy.106 = bf16[16,512,4,128]{3,1,2,0:T(8,128)(2,1)} copy(bf16[16,512,4,128]{1,3,2,0:T(8,128)(2,1)} %bitcast.121) | data formatting | bytes 16777216 | tf_op jit(solution)/shard_map/reshape | solution.py:77
  337.4 12.3 %copy.98 = bf16[16,512,512]{1,2,0:T(8,128)(2,1)} copy(bf16[16,512,512]{2,1,0:T(8,128)(2,1)} %get-tuple-element.243) | data formatting | bytes 16777216 | tf_op jit(solution)/shard_map/slice | solution.py:74
  349.7 12.3 %copy.99 = bf16[16,512,4,128]{3,1,2,0:T(8,128)(2,1)} copy(bf16[16,512,4,128]{1,3,2,0:T(8,128)(2,1)} %bitcast.122) | data formatting | bytes 16777216 | tf_op jit(solution)/shard_map/reshape | solution.py:74
  362.1 9.6 %bitcast_reduce_fusion = (f32[8,16,4,8]{3,0,2,1:T(8,128)S(1)}, f32[16,4,512,8,8]{2,4,3,1,0:T(8,128)}) fusion(pred[16,512]{1,0:T(8,128)(4,1)S(1)} %broadcast_compare_fusion, bf16[8,16,4,8,128]{4,3,2,1,0:T(8,128)(2,1)S(1)} %bitcast.125, bf16[16,512,4,128]{3,1,2,0:T(8,128)(2,1)} %copy.99), kind=kOutput, calls=%fused_computation.18 | convolution fusion | flops 543158272 | bytes 17850368 | tf_op jit(solution)/shard_map/sckgd,ckpd->sckgp/dot_general | solution.py:116
  371.7 8.8 %fusion.27 = bf16[8,16,4,8,128]{4,3,0,2,1:T(8,128)(2,1)} fusion(f32[16,4,512,8,8]{2,4,3,1,0:T(8,128)} %get-tuple-element.263, f32[8,16,4,8]{3,0,2,1:T(8,128)S(1)} %get-tuple-element.262, pred[16,512]{1,0:T(8,128)(4,1)S(1)} %broadcast_compare_fusion, bf16[16,512,4,128]{3,1,2,0:T(8,128)(2,1)} %copy.106), kind=kOutput, calls=%fused_computation.41 | convolution fusion | flops 547880960 | bytes 17850368 | tf_op jit(solution)/shard_map/sckgp,ckpd->sckgd/dot_general | solution.py:123
  380.6 1.6 fusion.18
  382.7 12.4 %all_gather.69 = bf16[8,16,512]{2,1,0:T(8,128)(2,1)S(1)} all-gather(bf16[8,16,128]{2,1,0:T(8,128)(2,1)S(1)} %bitcast.133), channel_id=1, replica_groups=mesh['parts'=2,'replica'=4,'tensor'=4] {'tensor'}, dimensions={2}, use_global_device_ids=true | all-gather | bytes 163840 | tf_op jit(solution)/shard_map/all_gather | solution.py:108
  395.1 0.7 reshape.255
  395.8 1.8 convolution_convert_fusion.2
  397.7 18.6 %all_gather.68 = bf16[8,16,512]{2,1,0:T(8,128)(2,1)S(1)} all-gather(bf16[8,16,128]{2,1,0:T(8,128)(2,1)S(1)} %bitcast.132), channel_id=1, replica_groups=mesh['parts'=2,'replica'=4,'tensor'=4] {'tensor'}, dimensions={2}, use_global_device_ids=true | all-gather | bytes 163840 | tf_op jit(solution)/shard_map/all_gather | solution.py:107
  416.9 6.1 %fusion.38 = f32[16,4,8,8,8]{4,2,3,1,0:T(8,128)} fusion(bf16[8,16,4,8,128]{4,3,2,1,0:T(8,128)(2,1)S(1)} %bitcast.126, bf16[8,16,4,64]{3,0,2,1:T(8,128)(2,1)S(1)} %get-tuple-element.247, bf16[8,16,4,64]{3,0,2,1:T(8,128)(2,1)S(1)} %get-tuple-element.246), kind=kOutput, calls=%fused_computation.52 | convolution fusion | flops 8650752 | bytes 1310720 | tf_op jit(solution)/shard_map/sckgd,tckd->sckgt/dot_general | solution.py:132
  423.0 2.6 copy.114
  426.1 1.3 fusion.41
  427.3 2.7 copy.121
  430.2 4.8 fusion.10
  435.2 16.7 %all-gather.9 = bf16[32,16,4,8]{1,3,2,0:T(8,128)(2,1)S(1)} all-gather(bf16[8,16,4,8]{1,3,2,0:T(8,128)(2,1)S(1)} %copy.104), channel_id=11, replica_groups=mesh['parts'=2,'replica'=4,'tensor'=4] {'tensor'}, dimensions={0}, use_global_device_ids=true | all-gather | bytes 40960 | tf_op jit(solution)/shard_map/all_gather | solution.py:18
  452.0 18.0 %all-gather.8 = bf16[32,16,4,8]{1,3,2,0:T(8,128)(2,1)S(1)} all-gather(bf16[8,16,4,8]{1,3,2,0:T(8,128)(2,1)S(1)} %copy.103), channel_id=10, replica_groups=mesh['parts'=2,'replica'=4,'tensor'=4] {'tensor'}, dimensions={0}, use_global_device_ids=true | all-gather | bytes 40960 | tf_op jit(solution)/shard_map/all_gather | solution.py:18
  470.0 0.7 slice_convert_fusion.1
  470.7 0.7 slice_convert_fusion.2
  472.0 1.5 slice_convert_fusion
  473.8 20.8 %while.19 = (s32[]{:T(128)}, f32[8,16,4,8]{1,3,2,0:T(8,128)}, f32[8,16,4,8]{1,3,2,0:T(8,128)}, f32[8,16,4,8,128]{4,3,2,1,0:T(8,128)S(1)}, bf16[4,8,16,4,8]{2,4,3...) while((s32[]{:T(128)}, f32[8,16,4,8]{1,3,2,0:T(8,128)}, ...), condition=%wide.region_4.5_spmd, body=%wide.region_3.4_spmd.sunk | while | flops 2129925 | bytes 5947535 | solution.py:26
  473.8 1.8 fusion.68
  475.6 1.7 copy.166
  477.3 0.8 copy.167
  478.2 2.5 fusion.69
  480.8 1.8 fusion.68
  482.5 1.7 copy.166
  484.3 0.8 copy.167
  485.1 2.5 fusion.69
  487.7 1.8 fusion.68
  489.5 1.7 copy.166
  491.2 0.8 copy.167
  492.1 2.5 fusion.69
  494.6 1.9 multiply_add_fusion
  496.5 1.8 copy.126
  498.3 1.9 copy.117
  500.2 0.9 copy.123
  501.1 3.2 fusion.21
  505.0 6.2 %convolution_convert_fusion = bf16[128,1280]{1,0:T(8,128)(2,1)} fusion(bf16[128,4096]{1,0:T(8,128)(2,1)S(1)} %convert_element_type.175, bf16[4096,1280]{1,0:T(8,128)(2,1)} %param.14), kind=kOutput, calls=%fused_computation.34 | convolution fusion | flops 1342341120 | bytes 11862016 | tf_op jit(solution)/shard_map/dot_general | solution.py:149
  (55 shorter events, 5.1 us)
Async XLA Ops:
  6.5 375.7 %copy-start = (bf16[5120,128]{1,0:T(8,128)(2,1)S(1)}, bf16[5120,128]{1,0:T(8,128)(2,1)}, u32[]{:S(2)}) copy-start(bf16[5120,128]{1,0:T(8,128)(2,1)} %param.13) | copy-start | bytes 3932164
  6.5 171.3 %all-gather.17.cloned.1.call-start = ((), (), s32[]{:S(2)}) async-start(), calls=%async_computation.1 | async-start | bytes 1310720 | tf_op jit(solution)/shard_map/all_gather | solution.py:106
  127.1 14.5 %copy-start.3 = (bf16[8,16,5120]{2,1,0:T(8,128)(2,1)}, bf16[8,16,5120]{2,1,0:T(8,128)(2,1)S(1)}, u32[]{:S(2)}) copy-start(bf16[8,16,5120]{2,1,0:T(8,128)(2,1)S(1)} %constant_dynamic-update-slice_fusion) | copy-start | bytes 3932164
  149.0 1.0 copy-start.7
  149.0 135.8 %all-gather.15.cloned.1.call-start = ((), (), s32[]{:S(2)}) async-start(), calls=%async_computation | async-start | bytes 20971520 | tf_op jit(solution)/shard_map/all_gather | solution.py:69
  149.8 322.2 %all-gather.19.cloned.1.call-start = ((), (), s32[]{:S(2)}) async-start(), calls=%async_computation.2 | async-start | bytes 5242880 | tf_op jit(solution)/shard_map/all_gather | solution.py:18
  179.3 182.7 %copy-start.1 = (bf16[16,8,32,128]{3,2,1,0:T(8,128)(2,1)}, bf16[16,8,32,128]{3,2,1,0:T(8,128)(2,1)S(1)}, u32[]{:S(2)}) copy-start(bf16[16,8,32,128]{3,2,1,0:T(8,128)(2,1)S(1)} %copy.142) | copy-start | bytes 3145732
  397.6 19.2 %copy-start.2 = (bf16[16,8,32,128]{3,2,1,0:T(8,128)(2,1)S(1)}, bf16[16,8,32,128]{3,2,1,0:T(8,128)(2,1)}, u32[]{:S(2)}) copy-start(bf16[16,8,32,128]{3,2,1,0:T(8,128)(2,1)} %copy-done.1) | copy-start | bytes 3145732
  426.1 9.0 %copy-start.6 = (f32[8,16,4,8]{1,3,2,0:T(8,128)}, f32[8,16,4,8]{1,3,2,0:T(8,128)S(1)}, u32[]{:S(2)}) copy-start(f32[8,16,4,8]{1,3,2,0:T(8,128)S(1)} %fusion.37) | copy-start | bytes 49156
  452.0 18.0 %copy-start.4 = (bf16[32,16,4,8]{1,3,2,0:T(8,128)(2,1)}, bf16[32,16,4,8]{1,3,2,0:T(8,128)(2,1)S(1)}, u32[]{:S(2)}) copy-start(bf16[32,16,4,8]{1,3,2,0:T(8,128)(2,1)S(1)} %all-gather.9) | copy-start | bytes 98308
  470.0 0.7 copy-start.5
Sparse Core Ops, SparseCore 0:
  149.1 28.6 all-gather.16
  179.4 105.4 all-gather.14
  380.6 91.3 all-gather.18
where the time goes:
time: 520 us; the launch traced here: 518 us
  blocking collectives  181 us (35%)
  waiting for transfers between devices  135 us (26%)
  local copies, waits for them, and re-layouts  108 us (21%)
  matrix products  42.5 us (8%)
  other arithmetic  37.3 us (7%)
  between operations  14.1 us (3%)
    all_gather x8, blocking collectives, per_device(): lax.all_gather(embedded[step], 'tensor', axis=1, tiled=True)  109 us
    all_gather x1, waiting for transfers between devices, per_device(): table = lax.all_gather(prefix_cache, 'replica', axis=0, tiled=True)  106 us
    all_gather x2, blocking collectives, combined_all(): lax.all_gather(part.astype(kind), axis)  34.7 us
    all_gather x1, waiting for transfers between devices, per_device(): lax.all_gather(query_part, 'tensor', axis=2, tiled=True)  27.8 us
    slice x2, local copies, waits for them, and re-layouts, per_device(): chosen[:, :, kv_width:].reshape(rows, pos_dev, KV_HEADS, HEAD)  18.6 us
    all_gather x1, blocking collectives, per_device(): lax.all_gather(key_part, 'tensor', axis=2, tiled=True)  18.6 us
    dot_general x1, local copies, waits for them, and re-layouts, per_device(): query_part = jnp.dot(normed, w_query, preferred_element_type=jnp.float32)  13.9 us
    gather x1, local copies, waits for them, and re-layouts, per_device(): chosen = jnp.take(table, child_parent, axis=0)  13 us
  transfers between devices with their start and end apart: 3, of which 3 were waited for; matrix products, arithmetic and copies ran while one was open for 5% of the time, Pallas kernels for 0%

commit v1 on v0

--- a/solution.py
+++ b/solution.py
@@ -1,6 +1,10 @@
+import functools
+
 import jax
 import jax.numpy as jnp
 from jax import lax
+from jax.experimental import pallas as pl
+from jax.experimental.pallas import tpu as pltpu
 from jax.sharding import PartitionSpec as P
 
 HEADS = 32
@@ -150,6 +154,506 @@
     return result.reshape(steps, rows, -1)
 
 
+GROUP = HEADS // KV_HEADS
+SCALE = HEAD ** (-0.5)
+MESH = pl.DeviceIdType.MESH
+
+
+def flip(index, step):
+    if step == 0:
+        return index
+    if step == 1:
+        return index + 1 - 2 * lax.rem(index, 2)
+    if step == 2:
+        return index + 2 - 4 * (index // 2)
+    return 3 - index
+
+
+def send(src, dst, sems, slot, device):
+    copy = pltpu.make_async_remote_copy(
+        src_ref=src,
+        dst_ref=dst,
+        send_sem=sems[0].at[slot],
+        recv_sem=sems[1].at[slot],
+        device_id=device,
+        device_id_type=MESH,
+    )
+    copy.start()
+    return copy
+
+
+def greet(devices):
+    barrier = pltpu.get_barrier_semaphore()
+    for device in devices:
+        pl.semaphore_signal(barrier, inc=1, device_id=device, device_id_type=MESH)
+    pl.semaphore_wait(barrier, len(devices))
+
+
+def compact(column, children, rows):
+    lane = lax.broadcasted_iota(jnp.int32, (rows, 128), 1)
+    out = jnp.zeros((rows, 128), jnp.float32)
+    for c in range(children):
+        out = jnp.where(lane == c, column[c * rows : (c + 1) * rows], out)
+    return out
+
+
+def project_kernel(
+    emb,
+    meta,
+    cpb,
+    freq,
+    wq,
+    wk,
+    wv,
+    cache,
+    q_own,
+    q_part,
+    kv_sib,
+    meta_all,
+    o_self,
+    l_self,
+    ebuf,
+    wqb,
+    wkb,
+    accq,
+    acck,
+    qsend,
+    e_s,
+    e_r,
+    w_s,
+    q_s,
+    q_r,
+    x_s,
+    x_r,
+    m_s,
+    m_r,
+    k_s,
+    k_r,
+    loc_s,
+):
+    part = lax.axis_index("parts")
+    r = lax.axis_index("replica")
+    t = lax.axis_index("tensor")
+    rows, width = emb.shape
+    children = q_own.shape[1]
+    steps = rows // children
+    par_dev = cache.shape[0]
+
+    def at(rep, ten):
+        return (part, rep, ten)
+
+    loads = []
+    for d in range(4):
+        k = flip(t, d)
+        span = pl.ds(pl.multiple_of(k * width, width), width)
+        loads.append(
+            (
+                pltpu.make_async_copy(wq.at[span], wqb.at[d], w_s.at[3 * d]),
+                pltpu.make_async_copy(
+                    wk.at[span], wkb.at[d, :, pl.ds(0, HEAD)], w_s.at[3 * d + 1]
+                ),
+                pltpu.make_async_copy(
+                    wv.at[span], wkb.at[d, :, pl.ds(HEAD, HEAD)], w_s.at[3 * d + 2]
+                ),
+            )
+        )
+        for load in loads[-1]:
+            load.start()
+    own_meta = pltpu.make_async_copy(meta, meta_all.at[0], loc_s.at[0])
+    own_meta.start()
+
+    greet([at(r, flip(t, d)) for d in (1, 2, 3)] + [at(flip(r, d), t) for d in (1, 2, 3)])
+    e_copies = [
+        send(emb, ebuf.at[d - 1], (e_s, e_r), d - 1, at(r, flip(t, d))) for d in (1, 2, 3)
+    ]
+    m_copies = [
+        send(meta, meta_all.at[d], (m_s, m_r), d - 1, at(flip(r, d), t)) for d in (1, 2, 3)
+    ]
+    kv_copy = send(cache, kv_sib, (k_s, k_r), 0, at(flip(r, 1), t))
+
+    own_meta.wait()
+    for copy in m_copies:
+        copy.wait_recv()
+    position = jnp.zeros((rows, 128), jnp.int32)
+    parents = cpb[...]
+    for d in range(4):
+        rep = flip(r, d)
+        table = meta_all[d]
+        for i in range(par_dev):
+            position = jnp.where(parents == rep * par_dev + i, table[i : i + 1, :], position)
+    step = lax.rem(lax.broadcasted_iota(jnp.int32, (rows, 128), 0), steps)
+    angle = (position + step).astype(jnp.float32) * freq[...]
+    cosine = jnp.cos(angle)
+    half = lax.broadcasted_iota(jnp.int32, (rows, 128), 1) < HEAD // 2
+    sine = jnp.sin(angle)
+    sine = jnp.where(half, -sine, sine)
+
+    squares = jnp.zeros((rows, 1), jnp.float32)
+    for d in range(4):
+        if d:
+            e_copies[d - 1].wait_recv()
+        block = emb[...] if d == 0 else ebuf[d - 1]
+        whole = block.astype(jnp.float32)
+        squares = squares + jnp.sum(whole * whole, axis=-1, keepdims=True)
+        for load in loads[d]:
+            load.wait()
+        more_q = jnp.dot(block, wqb[d], preferred_element_type=jnp.float32)
+        more_k = jnp.dot(block, wkb[d], preferred_element_type=jnp.float32)
+        if d == 0:
+            accq[...] = more_q
+            acck[...] = more_k
+        else:
+            accq[...] += more_q
+            acck[...] += more_k
+    norm = lax.rsqrt(squares / (4 * width) + EPS)
+
+    def turn(x):
+        return x * cosine + pltpu.roll(x, HEAD // 2, 1) * sine
+
+    def head_of(g):
+        x = turn(accq[:, g * HEAD : (g + 1) * HEAD] * norm)
+        return x.reshape(children, steps, HEAD)
+
+    for j in range(GROUP // 2):
+        pair = jnp.concatenate([head_of(2 * j), head_of(2 * j + 1)], axis=1)
+        qsend[:, 2 * steps * j : 2 * steps * (j + 1), :] = pair.astype(jnp.bfloat16)
+
+    own_q = pltpu.make_async_copy(qsend, q_own.at[t], loc_s.at[1])
+    own_q.start()
+    z_copies = [
+        send(qsend, q_own.at[t], (q_s, q_r), d - 1, at(r, flip(t, d))) for d in (1, 2, 3)
+    ]
+    x_copies = [send(qsend, q_part.at[t], (x_s, x_r), 0, at(flip(r, 2), t))]
+
+    key_raw = (acck[:, :HEAD] * norm).astype(jnp.bfloat16).astype(jnp.float32)
+    key_new = turn(key_raw).astype(jnp.bfloat16)
+    value = (acck[:, HEAD:] * norm).astype(jnp.bfloat16)
+    total_rows = children * GROUP * steps
+    scores = (
+        lax.dot_general(
+            qsend[...].reshape(total_rows, HEAD),
+            key_new,
+            (((1,), (1,)), ((), ())),
+            preferred_element_type=jnp.float32,
+        )
+        * SCALE
+    )
+    row = lax.broadcasted_iota(jnp.int32, (total_rows, rows), 0)
+    col = lax.broadcasted_iota(jnp.int32, (total_rows, rows), 1)
+    valid = (row // (GROUP * steps) == col // steps) & (lax.rem(col, steps) <= lax.rem(row, steps))
+    scores = jnp.where(valid, scores, NEG)
+    top = jnp.max(scores, axis=-1, keepdims=True)
+    weights = jnp.where(valid, jnp.exp(scores - top), 0.0)
+    total = jnp.sum(weights, axis=-1, keepdims=True)
+    summed = jnp.dot(weights.astype(jnp.bfloat16), value, preferred_element_type=jnp.float32)
+    o_self[...] = (summed / total).reshape(children, GROUP * steps, HEAD)
+    l_self[...] = compact(top + jnp.log(total), children, GROUP * steps)
+
+    for d in (1, 2, 3):
+        z_copies[d - 1].wait_recv()
+        k = flip(t, d)
+        x_copies.append(
+            send(q_own.at[k], q_part.at[k], (x_s, x_r), d, at(flip(r, 2), t))
+        )
+    own_q.wait()
+    for copy in x_copies:
+        copy.wait_recv()
+    kv_copy.wait_recv()
+    for copy in e_copies + m_copies + z_copies + x_copies + [kv_copy]:
+        copy.wait_send()
+
+
+def attend_kernel(meta_all, place, q_own, q_part, cache, kv_sib, o_own, l_own, o_part, l_part, kv, q, sems):
+    r = place[0]
+    t = place[1]
+    par_dev, block = cache.shape[0], cache.shape[1]
+    children, rows = o_own.shape[1], o_own.shape[2]
+    loads = [
+        pltpu.make_async_copy(cache, kv.at[pl.ds(0, par_dev)], sems.at[0]),
+        pltpu.make_async_copy(kv_sib, kv.at[pl.ds(par_dev, par_dev)], sems.at[1]),
+        pltpu.make_async_copy(q_own, q.at[0], sems.at[2]),
+        pltpu.make_async_copy(q_part, q.at[1], sems.at[3]),
+    ]
+    for load in loads:
+        load.start()
+    for ref in (o_own, l_own, o_part, l_part):
+        ref[...] = jnp.zeros(ref.shape, ref.dtype)
+    for load in loads:
+        load.wait()
+    lane = lax.broadcasted_iota(jnp.int32, (rows, 128), 1)
+    column = lax.broadcasted_iota(jnp.int32, (rows, block), 1) + t * block
+
+    for side, (o_ref, l_ref) in enumerate(((o_own, l_own), (o_part, l_part))):
+
+        def child(c, carry):
+            parent = meta_all[2 * side, 4, c]
+            owner = parent // par_dev
+            local = lax.rem(parent, par_dev)
+            away = jnp.where(owner == r, 0, 1)
+
+            @pl.when(owner // 2 == r // 2)
+            def _():
+                length = meta_all[away, local, 0]
+                slot = away * par_dev + local
+                valid = column < length
+                for k in range(KV_HEADS):
+                    keys = kv[slot, :, k * HEAD : (k + 1) * HEAD]
+                    values = kv[slot, :, (KV_HEADS + k) * HEAD : (KV_HEADS + k + 1) * HEAD]
+                    scores = (
+                        lax.dot_general(
+                            q[side, k, c],
+                            keys,
+                            (((1,), (1,)), ((), ())),
+                            preferred_element_type=jnp.float32,
+                        )
+                        * SCALE
+                    )
+                    scores = jnp.where(valid, scores, NEG)
+                    top = jnp.max(scores, axis=-1, keepdims=True)
+                    weights = jnp.where(valid, jnp.exp(scores - top), 0.0)
+                    total = jnp.sum(weights, axis=-1, keepdims=True)
+                    summed = jnp.dot(
+                        weights.astype(jnp.bfloat16), values, preferred_element_type=jnp.float32
+                    )
+                    some = total > 0.0
+                    safe = jnp.where(some, total, 1.0)
+                    o_ref[k, c] = (summed / safe).astype(jnp.bfloat16)
+                    lse = jnp.where(some, top + jnp.log(safe), NEG)
+                    l_ref[k] = jnp.where(lane == c, lse, l_ref[k])
+
+            return carry
+
+        lax.fori_loop(0, children, child, 0)
+
+
+def finish_kernel(
+    o_own,
+    l_own,
+    o_part,
+    l_part,
+    o_self,
+    l_self,
+    wo,
+    out,
+    rx_o,
+    rx_l,
+    mo,
+    ml,
+    ao,
+    al,
+    att,
+    abuf,
+    wob,
+    acc,
+    xo_s,
+    xo_r,
+    xl_s,
+    xl_r,
+    zo_s,
+    zo_r,
+    zl_s,
+    zl_r,
+    a_s,
+    a_r,
+    w_s,
+):
+    part = lax.axis_index("parts")
+    r = lax.axis_index("replica")
+    t = lax.axis_index("tensor")
+    children, rows = o_own.shape[1], o_own.shape[2]
+    steps = rows // GROUP
+    deep = GROUP * HEAD
+
+    def at(rep, ten):
+        return (part, rep, ten)
+
+    loads = []
+    for d in range(4):
+        k = flip(t, d)
+        loads.append(
+            pltpu.make_async_copy(
+                wo.at[pl.ds(pl.multiple_of(k * deep, deep), deep)], wob.at[d], w_s.at[d]
+            )
+        )
+        loads[-1].start()
+    greet([at(r, flip(t, d)) for d in (1, 2, 3)] + [at(flip(r, 2), t)])
+    order = (3, 2, 1, 0)
+    x_copies = {}
+    for d in order:
+        k = flip(t, d)
+        x_copies[d] = (
+            send(o_part.at[k], rx_o.at[d], (xo_s, xo_r), d, at(flip(r, 2), t)),
+            send(l_part.at[k], rx_l.at[d], (xl_s, xl_r), d, at(flip(r, 2), t)),
+        )
+    z_copies = {}
+    for d in order:
+        k = flip(t, d)
+        for copy in x_copies[d]:
+            copy.wait_recv()
+        mo[d] = o_own[k] + rx_o[d]
+        ml[d] = l_own[k] + rx_l[d]
+        if d:
+            z_copies[d] = (
+                send(mo.at[d], ao.at[d - 1], (zo_s, zo_r), d - 1, at(r, k)),
+                send(ml.at[d], al.at[d - 1], (zl_s, zl_r), d - 1, at(r, k)),
+            )
+    for d in (1, 2, 3):
+        for copy in z_copies[d]:
+            copy.wait_recv()
+    lses = [ml[0], l_self[...]] + [al[d] for d in range(3)]
+    top = functools.reduce(jnp.maximum, lses)
+    shares = [jnp.exp(lse - top) for lse in lses]
+    inverse = 1.0 / functools.reduce(jnp.add, shares)
+    shares = [share * inverse for share in shares]
+    for c in range(0, children, 2):
+        both = []
+        for one in (c, c + 1):
+            pieces = [mo[0, one], o_self[one]] + [ao[d, one] for d in range(3)]
+            mixed = jnp.zeros((rows, HEAD), jnp.float32)
+            for share, piece in zip(shares, pieces):
+                mixed = mixed + share[:, one : one + 1] * piece.astype(jnp.float32)
+            both.append(mixed)
+        for g in range(GROUP):
+            pair = jnp.concatenate([m[g * steps : (g + 1) * steps] for m in both], axis=0)
+            att[c * steps : (c + 2) * steps, g * HEAD : (g + 1) * HEAD] = pair.astype(jnp.bfloat16)
+    a_copies = [
+        send(att, abuf.at[d - 1], (a_s, a_r), d - 1, at(r, flip(t, d))) for d in (1, 2, 3)
+    ]
+    for d in range(4):
+        if d:
+            a_copies[d - 1].wait_recv()
+        block = att[...] if d == 0 else abuf[d - 1]
+        loads[d].wait()
+        more = jnp.dot(block, wob[d], preferred_element_type=jnp.float32)
+        if d == 0:
+            acc[...] = more
+        elif d < 3:
+            acc[...] += more
+        else:
+            out[...] = (acc[...] + more).astype(out.dtype)
+    for copy in a_copies:
+        copy.wait_send()
+    for d in range(4):
+        for copy in x_copies[d]:
+            copy.wait_send()
+        if d:
+            for copy in z_copies[d]:
+                copy.wait_send()
+
+
+def at_parents(embedded, w_query, w_key, w_value, w_out, prefix_cache, prefix_len, child_parent):
+    steps, children, width = embedded.shape
+    rows = steps * children
+    par_dev, block, kv_width = prefix_cache.shape
+    tall = GROUP * steps
+    out_width = w_out.shape[1]
+    bf16, f32, i32 = jnp.bfloat16, jnp.float32, jnp.int32
+    any_space = pl.BlockSpec(memory_space=pl.ANY)
+    vmem = pl.BlockSpec(memory_space=pltpu.VMEM)
+    smem = pl.BlockSpec(memory_space=pltpu.SMEM)
+    dma = pltpu.SemaphoreType.DMA
+    shape = jax.ShapeDtypeStruct
+
+    emb = jnp.transpose(embedded, (1, 0, 2)).reshape(rows, width)
+    lens = jnp.broadcast_to(prefix_len[:, None], (par_dev, 128))
+    names = jnp.pad(child_parent[None, :], ((0, 0), (0, 128 - children)))
+    meta = jnp.concatenate([lens, names, jnp.zeros((8 - par_dev - 1, 128), i32)], axis=0)
+    cpb = jnp.broadcast_to(jnp.repeat(child_parent, steps)[:, None], (rows, 128))
+    half = HEAD // 2
+    freq = ROPE_BASE ** (-jnp.arange(half, dtype=f32) / half)
+    freq = jnp.concatenate([freq, freq])[None, :]
+    place = jnp.stack([lax.axis_index("replica"), lax.axis_index("tensor")]).astype(i32)
+
+    q_own, q_part, kv_sib, meta_all, o_self, l_self = pl.pallas_call(
+        project_kernel,
+        out_shape=(
+            shape((KV_HEADS, children, tall, HEAD), bf16),
+            shape((KV_HEADS, children, tall, HEAD), bf16),
+            shape(prefix_cache.shape, bf16),
+            shape((4, 8, 128), i32),
+            shape((children, tall, HEAD), f32),
+            shape((tall, 128), f32),
+        ),
+        in_specs=[vmem, vmem, vmem, vmem, any_space, any_space, any_space, any_space],
+        out_specs=(any_space, any_space, any_space, vmem, vmem, vmem),
+        scratch_shapes=[
+            pltpu.VMEM((3, rows, width), bf16),
+            pltpu.VMEM((4, width, w_query.shape[1]), bf16),
+            pltpu.VMEM((4, width, 2 * HEAD), bf16),
+            pltpu.VMEM((rows, w_query.shape[1]), f32),
+            pltpu.VMEM((rows, 2 * HEAD), f32),
+            pltpu.VMEM((children, tall, HEAD), bf16),
+            dma((3,)),
+            dma((3,)),
+            dma((12,)),
+            dma((3,)),
+            dma((3,)),
+            dma((4,)),
+            dma((4,)),
+            dma((3,)),
+            dma((3,)),
+            dma((1,)),
+            dma((1,)),
+            dma((2,)),
+        ],
+        compiler_params=pltpu.CompilerParams(
+            collective_id=0, has_side_effects=True, vmem_limit_bytes=40 * 2**20
+        ),
+        name="project",
+    )(emb, meta, cpb, freq, w_query, w_key, w_value, prefix_cache)
+
+    values_shape = shape((KV_HEADS, children, tall, HEAD), bf16)
+    lse_shape = shape((KV_HEADS, tall, 128), f32)
+    o_own, l_own, o_part, l_part = pl.pallas_call(
+        attend_kernel,
+        out_shape=(values_shape, lse_shape, values_shape, lse_shape),
+        in_specs=[smem, smem, any_space, any_space, any_space, any_space],
+        out_specs=(vmem, vmem, vmem, vmem),
+        scratch_shapes=[
+            pltpu.VMEM((2 * par_dev, block, kv_width), bf16),
+            pltpu.VMEM((2, KV_HEADS, children, tall, HEAD), bf16),
+            dma((4,)),
+        ],
+        compiler_params=pltpu.CompilerParams(vmem_limit_bytes=40 * 2**20),
+        name="attend",
+    )(meta_all, place, q_own, q_part, prefix_cache, kv_sib)
+
+    result = pl.pallas_call(
+        finish_kernel,
+        out_shape=shape((rows, out_width), bf16),
+        in_specs=[vmem] * 6 + [any_space],
+        out_specs=vmem,
+        scratch_shapes=[
+            pltpu.VMEM((4, children, tall, HEAD), bf16),
+            pltpu.VMEM((4, tall, 128), f32),
+            pltpu.VMEM((4, children, tall, HEAD), bf16),
+            pltpu.VMEM((4, tall, 128), f32),
+            pltpu.VMEM((3, children, tall, HEAD), bf16),
+            pltpu.VMEM((3, tall, 128), f32),
+            pltpu.VMEM((rows, GROUP * HEAD), bf16),
+            pltpu.VMEM((3, rows, GROUP * HEAD), bf16),
+            pltpu.VMEM((4, GROUP * HEAD, out_width), bf16),
+            pltpu.VMEM((rows, out_width), f32),
+            dma((4,)),
+            dma((4,)),
+            dma((4,)),
+            dma((4,)),
+            dma((3,)),
+            dma((3,)),
+            dma((3,)),
+            dma((3,)),
+            dma((3,)),
+            dma((3,)),
+            dma((4,)),
+        ],
+        compiler_params=pltpu.CompilerParams(
+            collective_id=1, has_side_effects=True, vmem_limit_bytes=40 * 2**20
+        ),
+        name="finish",
+    )(o_own, l_own, o_part, l_part, o_self, l_self, w_out)
+    return jnp.transpose(result.reshape(children, steps, out_width), (1, 0, 2))
+
+
 def solution(mesh):
     in_specs = (
         P(None, ("parts", "replica"), "tensor"),
@@ -162,6 +666,8 @@
         P(("parts", "replica")),
     )
     out_specs = P(None, ("parts", "replica"), "tensor")
+    fits = mesh.shape["replica"] == 4 and mesh.shape["tensor"] == KV_HEADS
+    body = at_parents if fits else per_device
     return jax.shard_map(
-        per_device, mesh=mesh, in_specs=in_specs, out_specs=out_specs, check_vma=False
-    )
+        body, mesh=mesh, in_specs=in_specs, out_specs=out_specs, check_vma=False
+    )

time: 520 us -> 162 us (0.31)
  blocking collectives: 181 us -> 0 us
  Pallas kernels: 0 us -> 148 us
  waiting for transfers between devices: 135 us -> 0 us
  local copies, waits for them, and re-layouts: 108 us -> 12.3 us
  matrix products: 42.5 us -> 0 us
  other arithmetic: 37.3 us -> 0.89 us
  between operations: 14.1 us -> 0.06 us
    all_gather x12 -> x0, blocking collectives: 175 us -> none  [the longest x8 109 us: per_device(): lax.all_gather(embedded[step], 'tensor', axis=1, tiled=True)]
    pallas_call x0 -> x3, Pallas kernels: none -> 148 us  [the longest x1 70.2 us: at_parents(): pl.pallas_call(project_kernel, out_shape=(shape((KV_HEADS, children, tall...]
    all_gather x3 -> x0, waiting for transfers between devices: 134 us -> none  [the longest x1 106 us: per_device(): table = lax.all_gather(prefix_cache, 'replica', axis=0, tiled=True)]
    dot_general x8 -> x0, matrix products: 42.5 us -> none  [the longest x1 9.63 us: per_device(): jnp.einsum('sckgd,ckpd->sckgp', queries, keys, preferred_element_type=jnp...]
    slice x5 -> x0, local copies, waits for them, and re-layouts: 32.1 us -> none  [the longest x2 18.6 us: per_device(): chosen[:, :, kv_width:].reshape(rows, pos_dev, KV_HEADS, HEAD)]
    reshape x4 -> x1, local copies, waits for them, and re-layouts: 25.4 us -> 0.78 us  [at_parents(): return jnp.transpose(result.reshape(children, steps, out_width), (1, 0, 2))]
    dot_general x2 -> x0, local copies, waits for them, and re-layouts: 16.5 us -> none  [the longest x1 13.9 us: per_device(): query_part = jnp.dot(normed, w_query, preferred_element_type=jnp.float32)]
    add x8 -> x0, other arithmetic: 14.9 us -> none  [the longest x3 7.64 us: combine(): first[2] * left[..., None] + second[2] * right[..., None]]
  transfers between devices with their start and end apart: 3 -> 0, of which waited for: 3 -> 0; matrix products, arithmetic and copies ran while one was open for 5% -> 0% of each run, Pallas kernels for 0% -> 0%
where the time goes in v1:
time: 162 us
  Pallas kernels  148 us (91%)
  local copies, waits for them, and re-layouts  12.3 us (8%)
    pallas_call x1, Pallas kernels, at_parents(): pl.pallas_call(project_kernel, out_shape=(shape((KV_HEADS, children, tall...  70.2 us
    pallas_call x1, Pallas kernels, at_parents(): pl.pallas_call(finish_kernel, out_shape=shape((rows, out_width), bf16), i...  57.2 us
    pallas_call x1, Pallas kernels, at_parents(): pl.pallas_call(attend_kernel, out_shape=(values_shape, lse_shape, values_...  21 us
    unnamed x10, local copies, waits for them, and re-layouts  8.79 us

profile of v1, /device:TPU:0, one launch (start us, length us, event | category | flops | bytes accessed | tf_op | source)
XLA Modules:
  0.0 161.7 jit_solution(16503247134604999822)
XLA Ops:
  0.0 0.1 pad_add_fusion.1.place
  0.1 0.7 pad.9.clone
  0.7 0.1 pad.11.clone
  0.8 0.1 maximum_bitcast_fusion.freq
  0.9 0.7 fusion.meta
  1.6 0.7 broadcast_in_dim.28
  2.4 0.1 broadcast_in_dim.29
  2.4 0.1 broadcast_in_dim.30.cpb
  2.5 1.1 copy.16
  3.6 0.0 copy-start
  3.6 2.2 %copy-done = bf16[4,512,1024]{2,1,0:T(8,128)(2,1)S(1)} copy-done((bf16[4,512,1024]{2,1,0:T(8,128)(2,1)S(1)}, bf16[4,512,1024]{2,1,0:T(8,128)(2,1)}, u32[]{:S(2)}) %copy-start) | copy-done | bytes 4194328
  5.8 0.0 copy-start.3
  5.8 1.3 copy-done.3
  7.1 0.0 copy-start.4
  7.1 1.3 copy-done.4
  8.4 0.0 copy-start.1
  8.4 70.2 %project.1 = (bf16[4,16,64,128]{3,2,1,0:T(8,128)(2,1)S(1)}, bf16[4,16,64,128]{3,2,1,0:T(8,128)(2,1)S(1)}, bf16[4,512,1024]{2,1,0:T(8,128)(2,1)S(1)}, s32[4,8,128...) custom-call(bf16[128,1280]{1,0:T(8,128)(2,1)S(1)} %bitcast.13, s32[8,128]{1,0:T(8,128)S(1)} %fusion.meta, ...), custom_call_target="tpu_custom_call" | custom-call | tf_op jit(solution)/shard_map/project/pallas_call | solution.py:567
  78.7 0.0 copy-done.1
  78.7 21.0 %attend.1 = (bf16[4,16,64,128]{3,2,1,0:T(8,128)(2,1)S(1)}, f32[4,64,128]{2,1,0:T(8,128)S(1)}, bf16[4,16,64,128]{3,2,1,0:T(8,128)(2,1)S(1)}, f32[4,64,128]{2,1,0:T(8,128)S(1)}) custom-call(s32[4,8,128]{2,1,0:T(8,128)S(1)} %get-tuple-element.15.meta_all, s32[2]{0:T(128)S(1)} %pad_add_fusion.1.place, bf16[4,16,64,128]{3,2,1,0:T(8,128)(2,1)S(1)} %get-tuple-element.16.q_own, ...), custom_call_target="tpu_custom_call" | custom-call | tf_op jit(solution)/shard_map/attend/pallas_call | solution.py:607
  99.7 0.0 copy-start.2
  99.7 4.0 %copy-done.2 = bf16[4096,1280]{1,0:T(8,128)(2,1)S(1)} copy-done((bf16[4096,1280]{1,0:T(8,128)(2,1)S(1)}, bf16[4096,1280]{1,0:T(8,128)(2,1)}, u32[]{:S(2)}) %copy-start.2) | copy-done | bytes 10485784
  103.7 57.2 %finish.1 = bf16[128,1280]{1,0:T(8,128)(2,1)S(1)} custom-call(bf16[4,16,64,128]{3,2,1,0:T(8,128)(2,1)S(1)} %get-tuple-element.19.o_own, f32[4,64,128]{2,1,0:T(8,128)S(1)} %get-tuple-element.20.l_own, bf16[4,16,64,128]{3,2,1,0:T(8,128)(2,1)S(1)} %get-tuple-element.21.o_part, f32[4,64,128]{2,1,0:T(8,128)S(1)} %get-tuple-element.22.l_part, ...), custom_call_target="tpu_custom_call" | custom-call | tf_op jit(solution)/shard_map/finish/pallas_call | solution.py:621
  160.9 0.8 copy.15
  (2 shorter events, 0.0 us)
Async XLA Ops:
  3.6 2.2 %copy-start = (bf16[4,512,1024]{2,1,0:T(8,128)(2,1)S(1)}, bf16[4,512,1024]{2,1,0:T(8,128)(2,1)}, u32[]{:S(2)}) copy-start(bf16[4,512,1024]{2,1,0:T(8,128)(2,1)} %cache.3) | copy-start | bytes 12582916
  5.8 1.3 copy-start.3
  7.1 1.3 copy-start.4
  8.4 70.2 %copy-start.1 = (bf16[4,512,1024]{2,1,0:T(8,128)(2,1)S(1)}, bf16[4,512,1024]{2,1,0:T(8,128)(2,1)}, u32[]{:S(2)}) copy-start(bf16[4,512,1024]{2,1,0:T(8,128)(2,1)} %cache.3) | copy-start | bytes 12582916
  99.7 4.0 %copy-start.2 = (bf16[4096,1280]{1,0:T(8,128)(2,1)S(1)}, bf16[4096,1280]{1,0:T(8,128)(2,1)}, u32[]{:S(2)}) copy-start(bf16[4096,1280]{1,0:T(8,128)(2,1)} %wo.1) | copy-start | bytes 31457284

commit v2 on v0

--- a/solution.py
+++ b/solution.py
@@ -1,6 +1,10 @@
+import functools
+
 import jax
 import jax.numpy as jnp
 from jax import lax
+from jax.experimental import pallas as pl
+from jax.experimental.pallas import tpu as pltpu
 from jax.sharding import PartitionSpec as P
 
 HEADS = 32
@@ -150,6 +154,425 @@
     return result.reshape(steps, rows, -1)
 
 
+GROUP = HEADS // KV_HEADS
+SCALE = HEAD ** (-0.5)
+LOG2E = 1.4426950408889634
+UNROLL = 4
+MESH = pl.DeviceIdType.MESH
+
+
+def flip(index, step):
+    if step == 0:
+        return index
+    if step == 1:
+        return index + 1 - 2 * lax.rem(index, 2)
+    if step == 2:
+        return index + 2 - 4 * (index // 2)
+    return 3 - index
+
+
+def send(src, dst, sems, slot, device):
+    copy = pltpu.make_async_remote_copy(
+        src_ref=src,
+        dst_ref=dst,
+        send_sem=sems[0].at[slot],
+        recv_sem=sems[1].at[slot],
+        device_id=device,
+        device_id_type=MESH,
+    )
+    copy.start()
+    return copy
+
+
+def greet(devices):
+    barrier = pltpu.get_barrier_semaphore()
+    for device in devices:
+        pl.semaphore_signal(barrier, inc=1, device_id=device, device_id_type=MESH)
+    pl.semaphore_wait(barrier, len(devices))
+
+
+def compact(column, children, rows):
+    lane = lax.broadcasted_iota(jnp.int32, (rows, 128), 1)
+    out = jnp.zeros((rows, 128), jnp.float32)
+    for c in range(children):
+        out = jnp.where(lane == c, column[c * rows : (c + 1) * rows], out)
+    return out
+
+
+def forked_kernel(
+    lens,
+    names,
+    emb,
+    freq,
+    wq,
+    wk,
+    wv,
+    wo,
+    cache,
+    out,
+    meta,
+    metas,
+    meta_s,
+    ebuf,
+    wqb,
+    wkb,
+    wob,
+    accq,
+    acck,
+    kv,
+    q_own,
+    q_part,
+    o_own,
+    o_part,
+    l_part,
+    o_self,
+    rx_o,
+    rx_l,
+    mo,
+    ml,
+    ao,
+    al,
+    att,
+    abuf,
+    acc,
+    e_s,
+    e_r,
+    w_s,
+    wo_s,
+    q_s,
+    q_r,
+    x_s,
+    x_r,
+    m_s,
+    m_r,
+    k_s,
+    k_r,
+    loc_s,
+    xo_s,
+    xo_r,
+    xl_s,
+    xl_r,
+    zo_s,
+    zo_r,
+    zl_s,
+    zl_r,
+    a_s,
+    a_r,
+):
+    part = lax.axis_index("parts")
+    r = lax.axis_index("replica")
+    t = lax.axis_index("tensor")
+    rows, width = emb.shape
+    children, tall = q_own.shape[1], q_own.shape[2]
+    steps = rows // children
+    par_dev, block = cache.shape[0], cache.shape[1]
+    deep = GROUP * HEAD
+
+    def at(rep, ten):
+        return (part, rep, ten)
+
+    def local(src, dst, sem):
+        copy = pltpu.make_async_copy(src, dst, sem)
+        copy.start()
+        return copy
+
+    lane = lax.broadcasted_iota(jnp.int32, (8, 128), 1)
+    table = jnp.zeros((8, 128), jnp.int32)
+    for i in range(par_dev):
+        table = jnp.where(lane == i, lens[i], table)
+    for c in range(children):
+        table = jnp.where(lane == 16 + c, names[c], table)
+    meta[...] = table
+
+    loads = []
+    for d in range(4):
+        k = flip(t, d)
+        span = pl.ds(pl.multiple_of(k * width, width), width)
+        loads.append(
+            (
+                local(wq.at[span], wqb.at[d], w_s.at[3 * d]),
+                local(wk.at[span], wkb.at[d, :, pl.ds(0, HEAD)], w_s.at[3 * d + 1]),
+                local(wv.at[span], wkb.at[d, :, pl.ds(HEAD, HEAD)], w_s.at[3 * d + 2]),
+            )
+        )
+
+    greet([at(r, flip(t, d)) for d in (1, 2, 3)] + [at(flip(r, d), t) for d in (1, 2, 3)])
+    m_copies = [
+        send(meta, metas.at[d], (m_s, m_r), d - 1, at(flip(r, d), t)) for d in (1, 2, 3)
+    ]
+    e_copies = [
+        send(emb, ebuf.at[d - 1], (e_s, e_r), d - 1, at(r, flip(t, d))) for d in (3, 2, 1)
+    ][::-1]
+    kv_copy = send(
+        cache, kv.at[pl.ds(par_dev, par_dev)], (k_s, k_r), 0, at(flip(r, 1), t)
+    )
+    kv_own = local(cache, kv.at[pl.ds(0, par_dev)], loc_s.at[0])
+    metas[0] = table
+    for copy in m_copies:
+        copy.wait_recv()
+    meta_copy = local(metas, meta_s, loc_s.at[1])
+    out_loads = []
+    for d in range(4):
+        k = flip(t, d)
+        out_loads.append(
+            local(wo.at[pl.ds(pl.multiple_of(k * deep, deep), deep)], wob.at[d], wo_s.at[d])
+        )
+    meta_copy.wait()
+
+    def parent_of(side, c):
+        name = meta_s[2 * side, 0, 16 + c]
+        owner = lax.div(name, par_dev)
+        which = lax.rem(name, par_dev)
+        away = jnp.where(lax.rem(owner, 2) == lax.rem(r, 2), 0, 1)
+        other = jnp.where(lax.div(owner, 2) == lax.div(r, 2), 0, 1)
+        return other == 0, away * par_dev + which, meta_s[2 * other + away, 0, which]
+
+    step = lax.broadcasted_iota(jnp.int32, (steps, 128), 0)
+    position = jnp.concatenate([parent_of(0, c)[2] + step for c in range(children)], axis=0)
+    angle = position.astype(jnp.float32) * freq[...]
+    cosine = jnp.cos(angle)
+    half = lax.broadcasted_iota(jnp.int32, (rows, 128), 1) < HEAD // 2
+    sine = jnp.sin(angle)
+    sine = jnp.where(half, -sine, sine)
+
+    squares = jnp.zeros((rows, 1), jnp.float32)
+    for d in range(4):
+        if d:
+            e_copies[d - 1].wait_recv()
+        block_in = emb[...] if d == 0 else ebuf[d - 1]
+        whole = block_in.astype(jnp.float32)
+        squares = squares + jnp.sum(whole * whole, axis=-1, keepdims=True)
+        for load in loads[d]:
+            load.wait()
+        more_q = jnp.dot(block_in, wqb[d], preferred_element_type=jnp.float32)
+        more_k = jnp.dot(block_in, wkb[d], preferred_element_type=jnp.float32)
+        if d == 0:
+            accq[...] = more_q
+            acck[...] = more_k
+        else:
+            accq[...] += more_q
+            acck[...] += more_k
+    norm = lax.rsqrt(squares / (4 * width) + EPS)
+
+    def turn(x):
+        return x * cosine + pltpu.roll(x, HEAD // 2, 1) * sine
+
+    def head_of(g):
+        x = turn(accq[:, g * HEAD : (g + 1) * HEAD] * norm)
+        return x.reshape(children, steps, HEAD)
+
+    for j in range(GROUP // 2):
+        pair = jnp.concatenate([head_of(2 * j), head_of(2 * j + 1)], axis=1)
+        q_own[0, :, 2 * steps * j : 2 * steps * (j + 1), :] = pair.astype(jnp.bfloat16)
+
+    partner = at(flip(r, 2), t)
+    x_copies = [send(q_own.at[0], q_part.at[0], (x_s, x_r), 0, partner)]
+    z_copies = [
+        send(q_own.at[0], q_own.at[d], (q_s, q_r), d - 1, at(r, flip(t, d))) for d in (1, 2, 3)
+    ]
+
+    key_raw = (acck[:, :HEAD] * norm).astype(jnp.bfloat16).astype(jnp.float32)
+    key_new = turn(key_raw).astype(jnp.bfloat16)
+    value = (acck[:, HEAD:] * norm).astype(jnp.bfloat16)
+    total_rows = children * tall
+    scores = (
+        lax.dot_general(
+            q_own[0].reshape(total_rows, HEAD),
+            key_new,
+            (((1,), (1,)), ((), ())),
+            preferred_element_type=jnp.float32,
+        )
+        * SCALE
+    )
+    row = lax.broadcasted_iota(jnp.int32, (total_rows, rows), 0)
+    col = lax.broadcasted_iota(jnp.int32, (total_rows, rows), 1)
+    valid = (row // tall == col // steps) & (lax.rem(col, steps) <= lax.rem(row, steps))
+    scores = jnp.where(valid, scores, NEG)
+    top = jnp.max(scores, axis=-1, keepdims=True)
+    weights = jnp.where(valid, jnp.exp(scores - top), 0.0)
+    total = jnp.sum(weights, axis=-1, keepdims=True)
+    summed = jnp.dot(weights.astype(jnp.bfloat16), value, preferred_element_type=jnp.float32)
+    o_self[...] = (summed / total).reshape(children, tall, HEAD)
+    l_self = compact(top + jnp.log(total), children, tall)
+
+    kv_own.wait()
+    kv_copy.wait_recv()
+    column = lax.broadcasted_iota(jnp.int32, (tall, block), 1) + t * block
+    lanes = lax.broadcasted_iota(jnp.int32, (tall, 128), 1)
+
+    def attend(side, q, o_ref, head):
+        first = pl.multiple_of(head * HEAD, HEAD)
+        second = pl.multiple_of((KV_HEADS + head) * HEAD, HEAD)
+
+        def some(i, lses):
+            for u in range(UNROLL):
+                c = i * UNROLL + u
+                here, slot, length = parent_of(side, c)
+                seen = jnp.logical_and(here, length > t * block)
+                raw = lax.dot_general(
+                    q[c],
+                    kv[slot, :, pl.ds(first, HEAD)],
+                    (((1,), (1,)), ((), ())),
+                    preferred_element_type=jnp.float32,
+                )
+                raw = jnp.where(column < length, raw, NEG)
+                peak = jnp.max(raw, axis=-1, keepdims=True)
+                portion = jnp.exp2((raw - peak) * (SCALE * LOG2E))
+                sums = jnp.sum(portion, axis=-1, keepdims=True)
+                mixed = jnp.dot(
+                    portion.astype(jnp.bfloat16),
+                    kv[slot, :, pl.ds(second, HEAD)],
+                    preferred_element_type=jnp.float32,
+                )
+                o_ref[c] = jnp.where(seen, mixed / sums, 0.0).astype(jnp.bfloat16)
+                lse = jnp.where(seen, peak * SCALE + jnp.log(sums), NEG)
+                lse = jnp.where(here, lse, 0.0)
+                lses = jnp.where(lanes == c, lse, lses)
+            return lses
+
+        return lax.fori_loop(0, children // UNROLL, some, jnp.zeros((tall, 128), jnp.float32))
+
+    r_copies = []
+    t_copies = []
+
+    def merge(d):
+        for copy in r_copies[d]:
+            copy.wait_recv()
+        mo[d] = o_own[d] + rx_o[d]
+        ml[d] = ml[d] + rx_l[d]
+        if d:
+            t_copies.append(
+                (
+                    send(mo.at[d], ao.at[d - 1], (zo_s, zo_r), d - 1, at(r, flip(t, d))),
+                    send(ml.at[d], al.at[d - 1], (zl_s, zl_r), d - 1, at(r, flip(t, d))),
+                )
+            )
+
+    def forward(d):
+        z_copies[d - 1].wait_recv()
+        x_copies.append(send(q_own.at[d], q_part.at[d], (x_s, x_r), d, partner))
+
+    for d in range(4):
+        head = flip(t, d)
+        ml[d] = attend(0, q_own.at[d], o_own.at[d], head)
+        if d < 3:
+            forward(d + 1)
+        x_copies[d].wait_recv()
+        l_part[d] = attend(1, q_part.at[d], o_part.at[d], head)
+        r_copies.append(
+            (
+                send(o_part.at[d], rx_o.at[d], (xo_s, xo_r), d, partner),
+                send(l_part.at[d], rx_l.at[d], (xl_s, xl_r), d, partner),
+            )
+        )
+        if d:
+            merge(d - 1)
+    merge(3)
+
+    for copies in t_copies:
+        for copy in copies:
+            copy.wait_recv()
+    lses = [ml[0], l_self] + [al[d] for d in range(3)]
+    top = functools.reduce(jnp.maximum, lses)
+    shares = [jnp.exp(lse - top) for lse in lses]
+    inverse = 1.0 / functools.reduce(jnp.add, shares)
+    shares = [share * inverse for share in shares]
+    for c in range(0, children, 2):
+        both = []
+        for one in (c, c + 1):
+            pieces = [mo[0, one], o_self[one]] + [ao[d, one] for d in range(3)]
+            blend = jnp.zeros((tall, HEAD), jnp.float32)
+            for share, piece in zip(shares, pieces):
+                blend = blend + share[:, one : one + 1] * piece.astype(jnp.float32)
+            both.append(blend)
+        for g in range(GROUP):
+            pair = jnp.concatenate([m[g * steps : (g + 1) * steps] for m in both], axis=0)
+            att[c * steps : (c + 2) * steps, g * HEAD : (g + 1) * HEAD] = pair.astype(jnp.bfloat16)
+    a_copies = [
+        send(att, abuf.at[d - 1], (a_s, a_r), d - 1, at(r, flip(t, d))) for d in (3, 2, 1)
+    ][::-1]
+    for d in range(4):
+        if d:
+            a_copies[d - 1].wait_recv()
+        block_in = att[...] if d == 0 else abuf[d - 1]
+        out_loads[d].wait()
+        more = jnp.dot(block_in, wob[d], preferred_element_type=jnp.float32)
+        if d == 0:
+            acc[...] = more
+        elif d < 3:
+            acc[...] += more
+        else:
+            out[...] = (acc[...] + more).astype(out.dtype)
+    for copies in r_copies + t_copies:
+        for copy in copies:
+            copy.wait_send()
+    for copy in e_copies + m_copies + z_copies + x_copies + a_copies + [kv_copy]:
+        copy.wait_send()
+
+
+def at_parents(embedded, w_query, w_key, w_value, w_out, prefix_cache, prefix_len, child_parent):
+    steps, children, width = embedded.shape
+    rows = steps * children
+    par_dev, block, kv_width = prefix_cache.shape
+    tall = GROUP * steps
+    out_width = w_out.shape[1]
+    bf16, f32, i32 = jnp.bfloat16, jnp.float32, jnp.int32
+    any_space = pl.BlockSpec(memory_space=pl.ANY)
+    vmem = pl.BlockSpec(memory_space=pltpu.VMEM)
+    smem = pl.BlockSpec(memory_space=pltpu.SMEM)
+
+    emb = jnp.transpose(embedded, (1, 0, 2)).reshape(rows, width)
+    half = HEAD // 2
+    freq = ROPE_BASE ** (-jnp.arange(half, dtype=f32) / half)
+    freq = jnp.concatenate([freq, freq])[None, :]
+
+    def scratch(shape, kind=bf16):
+        return pltpu.VMEM(shape, kind)
+
+    result = pl.pallas_call(
+        forked_kernel,
+        out_shape=jax.ShapeDtypeStruct((rows, out_width), bf16),
+        in_specs=[smem, smem, vmem, vmem] + [any_space] * 5,
+        out_specs=vmem,
+        scratch_shapes=[
+            scratch((8, 128), i32),
+            scratch((4, 8, 128), i32),
+            pltpu.SMEM((4, 8, 128), i32),
+            scratch((3, rows, width)),
+            scratch((4, width, w_query.shape[1])),
+            scratch((4, width, 2 * HEAD)),
+            scratch((4, GROUP * HEAD, out_width)),
+            scratch((rows, w_query.shape[1]), f32),
+            scratch((rows, 2 * HEAD), f32),
+            scratch((2 * par_dev, block, kv_width)),
+            scratch((4, children, tall, HEAD)),
+            scratch((4, children, tall, HEAD)),
+            scratch((4, children, tall, HEAD)),
+            scratch((4, children, tall, HEAD)),
+            scratch((4, tall, 128), f32),
+            scratch((children, tall, HEAD), f32),
+            scratch((4, children, tall, HEAD)),
+            scratch((4, tall, 128), f32),
+            scratch((4, children, tall, HEAD)),
+            scratch((4, tall, 128), f32),
+            scratch((3, children, tall, HEAD)),
+            scratch((3, tall, 128), f32),
+            scratch((rows, GROUP * HEAD)),
+            scratch((3, rows, GROUP * HEAD)),
+            scratch((rows, out_width), f32),
+        ]
+        + [
+            pltpu.SemaphoreType.DMA((n,))
+            for n in (3, 3, 12, 4, 3, 3, 4, 4, 3, 3, 1, 1, 2, 4, 4, 4, 4, 3, 3, 3, 3, 3, 3)
+        ],
+        compiler_params=pltpu.CompilerParams(
+            collective_id=0, has_side_effects=True, vmem_limit_bytes=60 * 2**20
+        ),
+        name="forked",
+    )(prefix_len, child_parent, emb, freq, w_query, w_key, w_value, w_out, prefix_cache)
+    return jnp.transpose(result.reshape(children, steps, out_width), (1, 0, 2))
+
+
 def solution(mesh):
     in_specs = (
         P(None, ("parts", "replica"), "tensor"),
@@ -162,6 +585,8 @@
         P(("parts", "replica")),
     )
     out_specs = P(None, ("parts", "replica"), "tensor")
+    fits = mesh.shape["replica"] == 4 and mesh.shape["tensor"] == KV_HEADS
+    body = at_parents if fits else per_device
     return jax.shard_map(
-        per_device, mesh=mesh, in_specs=in_specs, out_specs=out_specs, check_vma=False
-    )
+        body, mesh=mesh, in_specs=in_specs, out_specs=out_specs, check_vma=False
+    )

time: 520 us -> 139 us (0.27)
  blocking collectives: 181 us -> 0 us
  waiting for transfers between devices: 135 us -> 0 us
  Pallas kernels: 0 us -> 134 us
  local copies, waits for them, and re-layouts: 108 us -> 3.55 us
  matrix products: 42.5 us -> 0 us
  other arithmetic: 37.3 us -> 0.68 us
  between operations: 14.1 us -> 0.01 us
    all_gather x12 -> x0, blocking collectives: 175 us -> none  [the longest x8 109 us: per_device(): lax.all_gather(embedded[step], 'tensor', axis=1, tiled=True)]
    pallas_call x0 -> x1, Pallas kernels: none -> 134 us  [at_parents(): pl.pallas_call(forked_kernel, out_shape=jax.ShapeDtypeStruct((rows, out_w...]
    all_gather x3 -> x0, waiting for transfers between devices: 134 us -> none  [the longest x1 106 us: per_device(): table = lax.all_gather(prefix_cache, 'replica', axis=0, tiled=True)]
    dot_general x8 -> x0, matrix products: 42.5 us -> none  [the longest x1 9.63 us: per_device(): jnp.einsum('sckgd,ckpd->sckgp', queries, keys, preferred_element_type=jnp...]
    slice x5 -> x0, local copies, waits for them, and re-layouts: 32.1 us -> none  [the longest x2 18.6 us: per_device(): chosen[:, :, kv_width:].reshape(rows, pos_dev, KV_HEADS, HEAD)]
    reshape x4 -> x1, local copies, waits for them, and re-layouts: 25.4 us -> 1.75 us  [at_parents(): return jnp.transpose(result.reshape(children, steps, out_width), (1, 0, 2))]
    dot_general x2 -> x0, local copies, waits for them, and re-layouts: 16.5 us -> none  [the longest x1 13.9 us: per_device(): query_part = jnp.dot(normed, w_query, preferred_element_type=jnp.float32)]
    add x8 -> x0, other arithmetic: 14.9 us -> none  [the longest x3 7.64 us: combine(): first[2] * left[..., None] + second[2] * right[..., None]]
  transfers between devices with their start and end apart: 3 -> 0, of which waited for: 3 -> 0; matrix products, arithmetic and copies ran while one was open for 5% -> 0% of each run, Pallas kernels for 0% -> 0%
where the time goes in v2:
time: 139 us
  Pallas kernels  134 us (96%)
  local copies, waits for them, and re-layouts  3.55 us (3%)
    pallas_call x1, Pallas kernels, at_parents(): pl.pallas_call(forked_kernel, out_shape=jax.ShapeDtypeStruct((rows, out_w...  134 us

profile of v2, /device:TPU:0, one launch (start us, length us, event | category | flops | bytes accessed | tf_op | source)
XLA Modules:
  0.0 138.5 jit_solution(16441919873623669726)
XLA Ops:
  0.0 0.7 maximum_bitcast_fusion.freq
  0.7 1.8 %copy.14 = bf16[16,8,1280]{2,1,0:T(8,128)(2,1)} copy(bf16[16,8,1280]{2,0,1:T(8,128)(2,1)} %bitcast.12) | data formatting | bytes 655360 | tf_op jit(solution)/shard_map/transpose | solution.py:524
  2.5 134.3 %forked.1 = bf16[128,1280]{1,0:T(8,128)(2,1)} custom-call(s32[4]{0:T(128)} %lens.1, s32[16]{0:T(128)} %names.1, bf16[128,1280]{1,0:T(8,128)(2,1)} %bitcast.11, f32[1,128]{1,0:T(1,128)} %maximum_bitcast_fusion.freq, bf16[5120,1024]{1,0:T(8,128)(2,1)} %wq.1, bf16[5120,128]{1,0:T(8,128)(2,1)} %wk.1, bf16[5120,128]{1,0:T(8,128)(2,1)} %wv.1, ...), custom_call_target="tpu_custom_call" | custom-call | tf_op jit(solution)/shard_map/forked/pallas_call | solution.py:532
  136.8 1.8 %copy.13 = bf16[16,8,1280]{2,0,1:T(8,128)(2,1)} copy(bf16[16,8,1280]{2,1,0:T(8,128)(2,1)} %bitcast.10) | data formatting | bytes 655360 | tf_op jit(solution)/shard_map/reshape | solution.py:573
  (1 shorter events, 0.0 us)

commit v3 on v2

--- a/solution.py
+++ b/solution.py
@@ -2,6 +2,7 @@
 
 import jax
 import jax.numpy as jnp
+import numpy as np
 from jax import lax
 from jax.experimental import pallas as pl
 from jax.experimental.pallas import tpu as pltpu
@@ -171,17 +172,62 @@
     return 3 - index
 
 
-def send(src, dst, sems, slot, device):
-    copy = pltpu.make_async_remote_copy(
+def remote(src, dst, sems, slot, device, landing=None):
+    return pltpu.make_async_remote_copy(
         src_ref=src,
         dst_ref=dst,
         send_sem=sems[0].at[slot],
-        recv_sem=sems[1].at[slot],
+        recv_sem=sems[1].at[slot if landing is None else landing],
         device_id=device,
         device_id_type=MESH,
     )
+
+
+def send(*args):
+    copy = remote(*args)
     copy.start()
     return copy
+
+
+def nth(t, i):
+    return (t, flip(t, 1), 2 - t // 2, 3 - 3 * (t // 2))[i]
+
+
+class LineGather:
+    def __init__(self, own, slots, sems, at, r, t):
+        self.middle = lax.rem((t + 1) // 2, 2) == 1
+        end, other = at(r, flip(t, 1)), at(r, 3 - t)
+        plan = (
+            (own, 1, end),
+            (own, 2, other),
+            (slots(1), 3, other),
+            (slots(2), 2, end),
+            (slots(3), 3, end),
+        )
+        self.copies = [
+            remote(src, slots(to), sems, n, device, to - 1)
+            for n, (src, to, device) in enumerate(plan)
+        ]
+        self.landings = [remote(slots(i), slots(i), sems, 0, end, i - 1) for i in (1, 2, 3)]
+        self.copies[0].start()
+        self.if_middle(self.copies[1].start)
+
+    def if_middle(self, act):
+        @pl.when(self.middle)
+        def _():
+            act()
+
+    def arrived(self, i):
+        self.landings[i - 1].wait_recv()
+        self.if_middle(self.copies[i + 1].start)
+
+    def finish(self):
+        self.copies[0].wait_send()
+
+        @pl.when(self.middle)
+        def _():
+            for copy in self.copies[1:]:
+                copy.wait_send()
 
 
 def greet(devices):
@@ -219,6 +265,7 @@
     wob,
     accq,
     acck,
+    heads,
     kv,
     q_own,
     q_part,
@@ -286,7 +333,7 @@
 
     loads = []
     for d in range(4):
-        k = flip(t, d)
+        k = nth(t, d)
         span = pl.ds(pl.multiple_of(k * width, width), width)
         loads.append(
             (
@@ -300,9 +347,7 @@
     m_copies = [
         send(meta, metas.at[d], (m_s, m_r), d - 1, at(flip(r, d), t)) for d in (1, 2, 3)
     ]
-    e_copies = [
-        send(emb, ebuf.at[d - 1], (e_s, e_r), d - 1, at(r, flip(t, d))) for d in (3, 2, 1)
-    ][::-1]
+    tokens = LineGather(emb, lambda i: ebuf.at[i - 1], (e_s, e_r), at, r, t)
     kv_copy = send(
         cache, kv.at[pl.ds(par_dev, par_dev)], (k_s, k_r), 0, at(flip(r, 1), t)
     )
@@ -313,7 +358,7 @@
     meta_copy = local(metas, meta_s, loc_s.at[1])
     out_loads = []
     for d in range(4):
-        k = flip(t, d)
+        k = nth(t, d)
         out_loads.append(
             local(wo.at[pl.ds(pl.multiple_of(k * deep, deep), deep)], wob.at[d], wo_s.at[d])
         )
@@ -338,7 +383,7 @@
     squares = jnp.zeros((rows, 1), jnp.float32)
     for d in range(4):
         if d:
-            e_copies[d - 1].wait_recv()
+            tokens.arrived(d)
         block_in = emb[...] if d == 0 else ebuf[d - 1]
         whole = block_in.astype(jnp.float32)
         squares = squares + jnp.sum(whole * whole, axis=-1, keepdims=True)
@@ -357,9 +402,15 @@
     def turn(x):
         return x * cosine + pltpu.roll(x, HEAD // 2, 1) * sine
 
+    def by_child(g, columns):
+        heads[g] = columns * norm
+        return jnp.concatenate(
+            [heads[g, pl.ds(c, steps, stride=children), :] for c in range(children)], axis=0
+        )
+
     def head_of(g):
-        x = turn(accq[:, g * HEAD : (g + 1) * HEAD] * norm)
-        return x.reshape(children, steps, HEAD)
+        x = by_child(g, accq[:, g * HEAD : (g + 1) * HEAD])
+        return turn(x).reshape(children, steps, HEAD)
 
     for j in range(GROUP // 2):
         pair = jnp.concatenate([head_of(2 * j), head_of(2 * j + 1)], axis=1)
@@ -367,13 +418,11 @@
 
     partner = at(flip(r, 2), t)
     x_copies = [send(q_own.at[0], q_part.at[0], (x_s, x_r), 0, partner)]
-    z_copies = [
-        send(q_own.at[0], q_own.at[d], (q_s, q_r), d - 1, at(r, flip(t, d))) for d in (1, 2, 3)
-    ]
-
-    key_raw = (acck[:, :HEAD] * norm).astype(jnp.bfloat16).astype(jnp.float32)
+    queries = LineGather(q_own.at[0], lambda i: q_own.at[i], (q_s, q_r), at, r, t)
+
+    key_raw = by_child(GROUP, acck[:, :HEAD]).astype(jnp.bfloat16).astype(jnp.float32)
     key_new = turn(key_raw).astype(jnp.bfloat16)
-    value = (acck[:, HEAD:] * norm).astype(jnp.bfloat16)
+    value = by_child(GROUP + 1, acck[:, HEAD:]).astype(jnp.bfloat16)
     total_rows = children * tall
     scores = (
         lax.dot_general(
@@ -441,22 +490,24 @@
         mo[d] = o_own[d] + rx_o[d]
         ml[d] = ml[d] + rx_l[d]
         if d:
+            seat = 0 if d == 1 else 2 - lax.rem((t + 1) // 2, 2)
+            device = at(r, nth(t, d))
             t_copies.append(
                 (
-                    send(mo.at[d], ao.at[d - 1], (zo_s, zo_r), d - 1, at(r, flip(t, d))),
-                    send(ml.at[d], al.at[d - 1], (zl_s, zl_r), d - 1, at(r, flip(t, d))),
+                    send(mo.at[d], ao.at[seat], (zo_s, zo_r), d - 1, device, seat),
+                    send(ml.at[d], al.at[seat], (zl_s, zl_r), d - 1, device, seat),
                 )
             )
 
     def forward(d):
-        z_copies[d - 1].wait_recv()
+        queries.arrived(d)
         x_copies.append(send(q_own.at[d], q_part.at[d], (x_s, x_r), d, partner))
 
     for d in range(4):
-        head = flip(t, d)
+        head = nth(t, d)
         ml[d] = attend(0, q_own.at[d], o_own.at[d], head)
-        if d < 3:
-            forward(d + 1)
+        if d == 0:
+            forward(1)
         x_copies[d].wait_recv()
         l_part[d] = attend(1, q_part.at[d], o_part.at[d], head)
         r_copies.append(
@@ -465,35 +516,33 @@
                 send(l_part.at[d], rx_l.at[d], (xl_s, xl_r), d, partner),
             )
         )
+        if d < 2:
+            forward(d + 2)
         if d:
             merge(d - 1)
     merge(3)
 
-    for copies in t_copies:
-        for copy in copies:
-            copy.wait_recv()
+    for seat in range(3):
+        remote(ao.at[seat], ao.at[seat], (zo_s, zo_r), seat, partner).wait_recv()
+        remote(al.at[seat], al.at[seat], (zl_s, zl_r), seat, partner).wait_recv()
     lses = [ml[0], l_self] + [al[d] for d in range(3)]
     top = functools.reduce(jnp.maximum, lses)
     shares = [jnp.exp(lse - top) for lse in lses]
     inverse = 1.0 / functools.reduce(jnp.add, shares)
     shares = [share * inverse for share in shares]
-    for c in range(0, children, 2):
-        both = []
-        for one in (c, c + 1):
-            pieces = [mo[0, one], o_self[one]] + [ao[d, one] for d in range(3)]
-            blend = jnp.zeros((tall, HEAD), jnp.float32)
-            for share, piece in zip(shares, pieces):
-                blend = blend + share[:, one : one + 1] * piece.astype(jnp.float32)
-            both.append(blend)
+    for c in range(children):
+        pieces = [mo[0, c], o_self[c]] + [ao[d, c] for d in range(3)]
+        blend = jnp.zeros((tall, HEAD), jnp.float32)
+        for share, piece in zip(shares, pieces):
+            blend = blend + share[:, c : c + 1] * piece.astype(jnp.float32)
         for g in range(GROUP):
-            pair = jnp.concatenate([m[g * steps : (g + 1) * steps] for m in both], axis=0)
-            att[c * steps : (c + 2) * steps, g * HEAD : (g + 1) * HEAD] = pair.astype(jnp.bfloat16)
-    a_copies = [
-        send(att, abuf.at[d - 1], (a_s, a_r), d - 1, at(r, flip(t, d))) for d in (3, 2, 1)
-    ][::-1]
+            heads[g, pl.ds(c, steps, stride=children), :] = blend[g * steps : (g + 1) * steps]
+    for g in range(GROUP):
+        att[:, g * HEAD : (g + 1) * HEAD] = heads[g].astype(jnp.bfloat16)
+    blends = LineGather(att, lambda i: abuf.at[i - 1], (a_s, a_r), at, r, t)
     for d in range(4):
         if d:
-            a_copies[d - 1].wait_recv()
+            blends.arrived(d)
         block_in = att[...] if d == 0 else abuf[d - 1]
         out_loads[d].wait()
         more = jnp.dot(block_in, wob[d], preferred_element_type=jnp.float32)
@@ -506,8 +555,10 @@
     for copies in r_copies + t_copies:
         for copy in copies:
             copy.wait_send()
-    for copy in e_copies + m_copies + z_copies + x_copies + a_copies + [kv_copy]:
+    for copy in m_copies + x_copies + [kv_copy]:
         copy.wait_send()
+    for gather in (tokens, queries, blends):
+        gather.finish()
 
 
 def at_parents(embedded, w_query, w_key, w_value, w_out, prefix_cache, prefix_len, child_parent):
@@ -521,10 +572,10 @@
     vmem = pl.BlockSpec(memory_space=pltpu.VMEM)
     smem = pl.BlockSpec(memory_space=pltpu.SMEM)
 
-    emb = jnp.transpose(embedded, (1, 0, 2)).reshape(rows, width)
+    emb = embedded.reshape(rows, width)
     half = HEAD // 2
-    freq = ROPE_BASE ** (-jnp.arange(half, dtype=f32) / half)
-    freq = jnp.concatenate([freq, freq])[None, :]
+    freq = np.float32(ROPE_BASE) ** (-np.arange(half, dtype=np.float32) / np.float32(half))
+    freq = jnp.asarray(np.concatenate([freq, freq])[None, :])
 
     def scratch(shape, kind=bf16):
         return pltpu.VMEM(shape, kind)
@@ -544,6 +595,7 @@
             scratch((4, GROUP * HEAD, out_width)),
             scratch((rows, w_query.shape[1]), f32),
             scratch((rows, 2 * HEAD), f32),
+            scratch((GROUP + 2, rows, HEAD), f32),
             scratch((2 * par_dev, block, kv_width)),
             scratch((4, children, tall, HEAD)),
             scratch((4, children, tall, HEAD)),
@@ -563,14 +615,14 @@
         ]
         + [
             pltpu.SemaphoreType.DMA((n,))
-            for n in (3, 3, 12, 4, 3, 3, 4, 4, 3, 3, 1, 1, 2, 4, 4, 4, 4, 3, 3, 3, 3, 3, 3)
+            for n in (5, 3, 12, 4, 5, 3, 4, 4, 3, 3, 1, 1, 2, 4, 4, 4, 4, 3, 3, 3, 3, 5, 3)
         ],
         compiler_params=pltpu.CompilerParams(
             collective_id=0, has_side_effects=True, vmem_limit_bytes=60 * 2**20
         ),
         name="forked",
     )(prefix_len, child_parent, emb, freq, w_query, w_key, w_value, w_out, prefix_cache)
-    return jnp.transpose(result.reshape(children, steps, out_width), (1, 0, 2))
+    return result.reshape(steps, children, out_width)
 
 
 def solution(mesh):

time: 139 us -> 122 us (0.88)
  Pallas kernels: 134 us -> 121 us
  local copies, waits for them, and re-layouts: 3.55 us -> 1.72 us
    pallas_call x1, Pallas kernels: 134 us -> 121 us  [at_parents(): pl.pallas_call(forked_kernel, out_shape=jax.ShapeDtypeStruct((rows, out_w...]
    transpose x1 -> x0, local copies, waits for them, and re-layouts: 1.79 us -> none  [at_parents(): emb = jnp.transpose(embedded, (1, 0, 2)).reshape(rows, width)]
    reshape x1 -> x0, local copies, waits for them, and re-layouts: 1.75 us -> none  [at_parents(): return jnp.transpose(result.reshape(children, steps, out_width), (1, 0, 2))]
    unnamed x0 -> x1, local copies, waits for them, and re-layouts: none -> 1.72 us
where the time goes in v3:
time: 122 us
  Pallas kernels  121 us (99%)
  local copies, waits for them, and re-layouts  1.72 us (1%)
    pallas_call x1, Pallas kernels, at_parents(): pl.pallas_call(forked_kernel, out_shape=jax.ShapeDtypeStruct((rows, out_w...  121 us

profile of v3, /device:TPU:0, one launch (start us, length us, event | category | flops | bytes accessed | tf_op | source)
XLA Modules:
  0.0 122.3 jit_solution(10083356502743098971)
XLA Ops:
  0.0 120.6 %forked.1 = bf16[128,1280]{1,0:T(8,128)(2,1)} custom-call(s32[4]{0:T(128)} %lens.1, s32[16]{0:T(128)} %names.1, bf16[128,1280]{1,0:T(8,128)(2,1)} %bitcast.3, f32[1,128]{1,0:T(1,128)} %constant.2.clone.freq, bf16[5120,1024]{1,0:T(8,128)(2,1)} %wq.1, bf16[5120,128]{1,0:T(8,128)(2,1)} %wk.1, bf16[5120,128]{1,0:T(8,128)(2,1)} %wv.1, bf16[4096,1280]{1,0:T(8,128)(2,1)} %wo.1, ...), custom_call_target="tpu_custom_call" | custom-call | tf_op jit(solution)/shard_map/forked/pallas_call | solution.py:583
  120.6 1.7 %copy.11 = bf16[8,16,1280]{2,1,0:T(8,128)(2,1)} copy(bf16[8,16,1280]{2,1,0:T(8,128)(2,1)} %bitcast.2) | data formatting | bytes 655360

commit v4 on v3

--- a/solution.py
+++ b/solution.py
@@ -481,7 +481,7 @@
 
         return lax.fori_loop(0, children // UNROLL, some, jnp.zeros((tall, 128), jnp.float32))
 
-    r_copies = []
+    r_copies = {}
     t_copies = []
 
     def merge(d):
@@ -503,24 +503,35 @@
         queries.arrived(d)
         x_copies.append(send(q_own.at[d], q_part.at[d], (x_s, x_r), d, partner))
 
-    for d in range(4):
-        head = nth(t, d)
-        ml[d] = attend(0, q_own.at[d], o_own.at[d], head)
-        if d == 0:
-            forward(1)
-        x_copies[d].wait_recv()
-        l_part[d] = attend(1, q_part.at[d], o_part.at[d], head)
-        r_copies.append(
-            (
-                send(o_part.at[d], rx_o.at[d], (xo_s, xo_r), d, partner),
-                send(l_part.at[d], rx_l.at[d], (xl_s, xl_r), d, partner),
-            )
+    def own_side(d):
+        ml[d] = attend(0, q_own.at[d], o_own.at[d], nth(t, d))
+
+    def partner_side(d):
+        l_part[d] = attend(1, q_part.at[d], o_part.at[d], nth(t, d))
+        r_copies[d] = (
+            send(o_part.at[d], rx_o.at[d], (xo_s, xo_r), d, partner),
+            send(l_part.at[d], rx_l.at[d], (xl_s, xl_r), d, partner),
         )
-        if d < 2:
-            forward(d + 2)
-        if d:
-            merge(d - 1)
+
+    own_side(0)
+    forward(1)
+    own_side(1)
+    x_copies[1].wait_recv()
+    forward(2)
+    partner_side(1)
+    own_side(2)
+    x_copies[2].wait_recv()
+    forward(3)
+    partner_side(2)
+    own_side(3)
+    merge(1)
+    x_copies[3].wait_recv()
+    partner_side(3)
+    x_copies[0].wait_recv()
+    partner_side(0)
+    merge(2)
     merge(3)
+    merge(0)
 
     for seat in range(3):
         remote(ao.at[seat], ao.at[seat], (zo_s, zo_r), seat, partner).wait_recv()
@@ -552,7 +563,7 @@
             acc[...] += more
         else:
             out[...] = (acc[...] + more).astype(out.dtype)
-    for copies in r_copies + t_copies:
+    for copies in list(r_copies.values()) + t_copies:
         for copy in copies:
             copy.wait_send()
     for copy in m_copies + x_copies + [kv_copy]:

time: 122 us -> 121 us (level)
  Pallas kernels: 121 us -> 119 us
    pallas_call x1, Pallas kernels: 121 us -> 119 us  [at_parents(): pl.pallas_call(forked_kernel, out_shape=jax.ShapeDtypeStruct((rows, out_w...]
where the time goes in v4:
time: 121 us; the launch traced here: 120 us
  Pallas kernels  119 us (98%)
  local copies, waits for them, and re-layouts  1.72 us (1%)
    pallas_call x1, Pallas kernels, at_parents(): pl.pallas_call(forked_kernel, out_shape=jax.ShapeDtypeStruct((rows, out_w...  119 us

profile of v4, /device:TPU:0, one launch (start us, length us, event | category | flops | bytes accessed | tf_op | source)
XLA Modules:
  0.0 120.4 jit_solution(2176848974341059628)
XLA Ops:
  0.0 118.7 %forked.1 = bf16[128,1280]{1,0:T(8,128)(2,1)} custom-call(s32[4]{0:T(128)} %lens.1, s32[16]{0:T(128)} %names.1, bf16[128,1280]{1,0:T(8,128)(2,1)} %bitcast.3, f32[1,128]{1,0:T(1,128)} %constant.2.clone.freq, bf16[5120,1024]{1,0:T(8,128)(2,1)} %wq.1, bf16[5120,128]{1,0:T(8,128)(2,1)} %wk.1, bf16[5120,128]{1,0:T(8,128)(2,1)} %wv.1, bf16[4096,1280]{1,0:T(8,128)(2,1)} %wo.1, ...), custom_call_target="tpu_custom_call" | custom-call | tf_op jit(solution)/shard_map/forked/pallas_call | solution.py:594
  118.7 1.7 %copy.11 = bf16[8,16,1280]{2,1,0:T(8,128)(2,1)} copy(bf16[8,16,1280]{2,1,0:T(8,128)(2,1)} %bitcast.2) | data formatting | bytes 655360
